TPU v7x, 256 devices: a whole 4x4x8 slice. The times are simulated.
256 devices in a mesh: expert: 4 (over z_hi), grid: 16 (over x, z_lo, core), layer: 4 (over y).
Axes of the slice: x: 4, y: 4, z: 8 (z_hi: 4, z_lo: 2; z = z_hi * 2 + z_lo), core: 2. Of those that a mesh axis runs over, the one named last changes fastest.
Arguments:
- iterate: bfloat16 [12288, 8192], P(('expert', 'grid'), 'layer'), parts along dimension 0, may hold values from -6 to 6
Outputs:
- new_iterate: bfloat16 [12288, 8192], P(('expert', 'grid'), 'layer'), parts along dimension 0
There are 4 independent parts, one for each index of `expert`. A program takes and returns all parts, laid end to end along the dimension named above; each array names one. Nothing has to cross between parts.
All inputs are finite; a program needn't handle non-finite values.
Results may differ from a plain program's by a relative error of at most 0.03.
Values may be sent and summed in bfloat16 or wider, within the bound.
A program may use at most 64 MiB of HBM per device.

v0:
```python
import jax
import jax.numpy as jnp
from jax import lax
from jax.sharding import PartitionSpec as P

N = 8192


linear_coef = 3.4445
cubic_coef = -4.775
quintic_coef = 2.0315


def body(iterate):
    inverse_n = 1.0 / N
    partial_value = (
        jnp.einsum(
            "ik,jk->ij",
            iterate,
            lax.all_gather(iterate, "grid", axis=0, tiled=True),
            preferred_element_type=jnp.float32,
        )
        * inverse_n
    )
    gram_part = lax.psum_scatter(
        partial_value.astype(jnp.bfloat16), "layer", scatter_dimension=1, tiled=True
    ).astype(jnp.float32)
    gram_low = gram_part.astype(jnp.bfloat16)
    square_partial = jnp.einsum(
        "ik,jk->ij",
        gram_low,
        lax.all_gather(gram_low, "grid", axis=0, tiled=True),
        preferred_element_type=jnp.float32,
    )
    square_part = lax.psum_scatter(
        square_partial.astype(jnp.bfloat16), "layer", scatter_dimension=1, tiled=True
    ).astype(jnp.float32)
    mixed_part = (cubic_coef * gram_part + quintic_coef * square_part).astype(jnp.bfloat16)
    mixed_full = lax.all_gather(mixed_part, "layer", axis=1, tiled=True)
    product = jnp.dot(
        mixed_full,
        lax.all_gather(iterate, "grid", axis=0, tiled=True),
        preferred_element_type=jnp.float32,
    )
    return (linear_coef * iterate.astype(jnp.float32) + product).astype(jnp.bfloat16)


def solution(mesh):
    in_specs = (P(("expert", "grid"), "layer"),)
    out_specs = P(("expert", "grid"), "layer")
    return jax.shard_map(body, mesh=mesh, in_specs=in_specs, out_specs=out_specs, check_vma=False)
```

profile of v0, /device:TPU:1, one launch (start us, length us, event | category | flops | bytes accessed | tf_op | source)
XLA Modules:
  0.0 242.6 jit_solution(11148297198453464893)
XLA Ops:
  6.5 0.0 all-gather.4.cloned.1.call-start
  6.5 0.7 all-gather.4.cloned.1.call-update
  7.3 0.0 reduce-scatter.3.cloned.1.call-start
  7.3 80.6 %all-gather.4.cloned.1.call-done = bf16[3072,2048]{1,0:T(8,128)(2,1)} async-done(((bf16[192,2048]{1,0:T(8,128)(2,1)}), bf16[3072,2048]{1,0:T(8,128)(2,1)}) %all-gather.4.cloned.1.call-update) | async-done | bytes 12582928 | tf_op jit(solution)/shard_map/all_gather | solution.py:20
  87.9 10.2 %fusion = bf16[192,3072]{1,0:T(8,128)(2,1)} fusion(bf16[192,2048]{1,0:T(8,128)(2,1)} %param.1, bf16[3072,2048]{1,0:T(8,128)(2,1)} %all-gather.4.cloned.1.call-done), kind=kOutput, calls=%fused_computation.1 | convolution fusion | flops 2417098752 | bytes 14548992 | tf_op jit(solution)/shard_map/ik,jk->ij/dot_general | solution.py:17
  98.1 0.0 reduce-scatter.3.cloned.1.call-update
  98.1 0.0 all-gather.6.cloned.1.call-start
  98.2 25.9 %reduce-scatter.3.cloned.1.call-done = bf16[192,768]{1,0:T(8,128)(2,1)} async-done(((bf16[192,3072]{1,0:T(8,128)(2,1)}), bf16[192,768]{1,0:T(8,128)(2,1)}) %reduce-scatter.3.cloned.1.call-update) | async-done | bytes 294928 | tf_op jit(solution)/shard_map/reduce_scatter | solution.py:25
  124.1 0.0 all-gather.6.cloned.1.call-update
  124.1 0.0 copy-start
  124.2 0.0 reduce-scatter.5.cloned.1.call-start
  124.2 44.1 %all-gather.6.cloned.1.call-done = bf16[3072,768]{1,0:T(8,128)(2,1)} async-done(((bf16[192,768]{1,0:T(8,128)(2,1)}), bf16[3072,768]{1,0:T(8,128)(2,1)}) %all-gather.6.cloned.1.call-update) | async-done | bytes 4718608 | tf_op jit(solution)/shard_map/all_gather | solution.py:32
  168.3 5.1 %convolution_convert_fusion = bf16[192,3072]{1,0:T(8,128)(2,1)} fusion(bf16[192,768]{1,0:T(8,128)(2,1)} %reduce-scatter.3.cloned.1.call-done, bf16[3072,768]{1,0:T(8,128)(2,1)} %all-gather.6.cloned.1.call-done), kind=kOutput, calls=%fused_computation.2 | convolution fusion | flops 906559488 | bytes 6193152 | tf_op jit(solution)/shard_map/ik,jk->ij/dot_general | solution.py:29
  173.4 0.0 copy-start.1
  173.5 0.0 reduce-scatter.5.cloned.1.call-update
  173.5 0.0 all-gather.8.cloned.1.call-start
  173.5 25.1 %reduce-scatter.5.cloned.1.call-done = bf16[192,768]{1,0:T(8,128)(2,1)} async-done(((bf16[192,3072]{1,0:T(8,128)(2,1)}), bf16[192,768]{1,0:T(8,128)(2,1)}) %reduce-scatter.5.cloned.1.call-update) | async-done | bytes 294928 | tf_op jit(solution)/shard_map/reduce_scatter | solution.py:35
  198.6 0.0 copy-done
  198.6 1.8 add_convert_fusion
  200.4 0.0 all-gather.8.cloned.1.call-update
  200.4 27.1 %all-gather.8.cloned.1.call-done = bf16[192,3072]{1,0:T(8,128)(2,1)} async-done(((bf16[192,768]{1,0:T(8,128)(2,1)}), bf16[192,3072]{1,0:T(8,128)(2,1)}) %all-gather.8.cloned.1.call-update) | async-done | bytes 1179664 | tf_op jit(solution)/shard_map/all_gather | solution.py:39
  227.6 0.0 copy-done.1
  227.6 8.4 %fusion.1 = bf16[192,2048]{1,0:T(8,128)(2,1)} fusion(bf16[192,3072]{1,0:T(8,128)(2,1)} %all-gather.8.cloned.1.call-done, bf16[3072,2048]{1,0:T(8,128)(2,1)} %all-gather.4.cloned.1.call-done, bf16[192,2048]{1,0:T(8,128)(2,1)S(1)} %copy-done.1), kind=kOutput, calls=%fused_computation.4 | convolution fusion | flops 2417491968 | bytes 15335424 | tf_op jit(solution)/shard_map/dot_general | solution.py:40
Async XLA Ops:
  6.5 81.4 %all-gather.4.cloned.1.call-start = ((), (), s32[]{:S(2)}) async-start(), calls=%async_computation.2 | async-start | bytes 13369344 | tf_op jit(solution)/shard_map/all_gather | solution.py:20
  7.3 116.9 %reduce-scatter.3.cloned.1.call-start = ((), (), s32[]{:S(2)}) async-start(), calls=%async_computation.3 | async-start | bytes 1474560 | tf_op jit(solution)/shard_map/reduce_scatter | solution.py:25
  98.1 70.2 %all-gather.6.cloned.1.call-start = ((), (), s32[]{:S(2)}) async-start(), calls=%async_computation.4 | async-start | bytes 5013504 | tf_op jit(solution)/shard_map/all_gather | solution.py:32
  124.1 74.5 %copy-start = (bf16[192,768]{1,0:T(8,128)(2,1)S(1)}, bf16[192,768]{1,0:T(8,128)(2,1)}, u32[]{:S(2)}) copy-start(bf16[192,768]{1,0:T(8,128)(2,1)} %reduce-scatter.3.cloned.1.call-done) | copy-start | bytes 884740
  124.2 74.5 %reduce-scatter.5.cloned.1.call-start = ((), (), s32[]{:S(2)}) async-start(), calls=%async_computation.5 | async-start | bytes 1474560 | tf_op jit(solution)/shard_map/reduce_scatter | solution.py:35
  173.4 54.1 %copy-start.1 = (bf16[192,2048]{1,0:T(8,128)(2,1)S(1)}, bf16[192,2048]{1,0:T(8,128)(2,1)}, u32[]{:S(2)}) copy-start(bf16[192,2048]{1,0:T(8,128)(2,1)} %param.1) | copy-start | bytes 2359300
  173.5 54.1 %all-gather.8.cloned.1.call-start = ((), (), s32[]{:S(2)}) async-start(), calls=%async_computation.6 | async-start | bytes 1474560 | tf_op jit(solution)/shard_map/all_gather | solution.py:39
Sparse Core Ops, SparseCore 0:
  9.2 78.6 all-gather.3
  98.3 25.8 reduce-scatter.2
  126.0 42.2 all-gather.5
  173.6 24.9 reduce-scatter.4
  200.6 26.9 all-gather.7
where the time goes:
time: 243 us
  waiting for transfers between devices  204 us (84%)
  matrix products  23.8 us (10%)
  between operations  13.1 us (5%)
    all_gather x1, waiting for transfers between devices, body(): lax.all_gather(iterate, 'grid', axis=0, tiled=True)  80.6 us
    all_gather x1, waiting for transfers between devices, body(): lax.all_gather(gram_low, 'grid', axis=0, tiled=True)  44.1 us
    all_gather x1, waiting for transfers between devices, body(): mixed_full = lax.all_gather(mixed_part, 'layer', axis=1, tiled=True)  27.1 us
    reduce_scatter x1, waiting for transfers between devices, body(): lax.psum_scatter(partial_value.astype(jnp.bfloat16), 'layer', scatter_dim...  25.9 us
    reduce_scatter x1, waiting for transfers between devices, body(): lax.psum_scatter(square_partial.astype(jnp.bfloat16), 'layer', scatter_di...  25.1 us
    dot_general x1, matrix products, body(): jnp.einsum('ik,jk->ij', iterate, lax.all_gather(iterate, 'grid', axis=0,...  10.2 us
    dot_general x1, matrix products, body(): jnp.dot(mixed_full, lax.all_gather(iterate, 'grid', axis=0, tiled=True),...  8.45 us
    dot_general x1, matrix products, body(): jnp.einsum('ik,jk->ij', gram_low, lax.all_gather(gram_low, 'grid', axis=0...  5.15 us
  transfers between devices with their start and end apart: 5, of which 5 were waited for; matrix products, arithmetic and copies ran while one was open for 0% of the time, Pallas kernels for 0%

commit v1 on v0

v1 whole, which is shorter than its diff:
```python
import functools

import jax
import jax.numpy as jnp
from jax import lax
from jax.experimental import pallas as pl
from jax.experimental.pallas import tpu as pltpu
from jax.sharding import PartitionSpec as P

MESH = pl.DeviceIdType.MESH

LINEAR = 3.4445
CUBIC = -4.775
QUINTIC = 2.0315

NX = 4
NY = 4
SHIFTS = (0, 1, 3, 2)
CHUNKS = 3


def kernel(n_cols, x_ref, o_ref, rows, send, part, got, gram, g32, sq, sgot, mixed, ypart, yrem, ssem, rsem, lsem):
    half, width = x_ref.shape[0] // 2, x_ref.shape[1]
    quarter = half
    chunk = quarter // CHUNKS
    block = 4 * half
    expert, grid, y = lax.axis_index("expert"), lax.axis_index("grid"), lax.axis_index("layer")
    x, z, c = grid // 4, (grid // 2) % 2, grid % 2
    home = c == z

    def at(x_to=None, z_to=None, c_to=None, y_to=None):
        gx = x if x_to is None else x_to
        gz = z if z_to is None else z_to
        gc = c if c_to is None else c_to
        return (expert, gx * 4 + gz * 2 + gc, y if y_to is None else y_to)

    def around(base, step):
        return (base + step) % 4

    right, left = at(x_to=around(x, 1)), at(x_to=around(x, 3))
    sibling = at(c_to=1 - c)
    across = at(z_to=1 - z, c_to=z)
    along_y = [at(y_to=around(y, step)) for step in (1, 2, 3)]

    barrier = pltpu.get_barrier_semaphore()
    greeted = [right, left, sibling, at(z_to=1 - z), at(z_to=1 - z, c_to=1 - c)] + along_y
    for device in greeted:
        pl.semaphore_signal(barrier, inc=1, device_id=device, device_id_type=MESH)
    pl.semaphore_wait(barrier, len(greeted))

    used = [0, 0]
    pending = []

    def slots(count=1):
        used[1] += count
        return used[1] - count

    def copy(src, dst, device, slot):
        used[0] += 1
        made = pltpu.make_async_remote_copy(
            src_ref=src, dst_ref=dst, send_sem=ssem.at[used[0] - 1], recv_sem=rsem.at[slot],
            device_id=device, device_id_type=MESH,
        )
        return made

    def push(src, dst, device, slot=None):
        made = copy(src, dst, device, slots() if slot is None else slot)
        made.start()
        pending.append(made)
        return made

    def x_block(core_half):
        return x_ref.at[pl.ds(core_half * half, half), :]

    from_left = [None, None]
    from_right = [None, None]
    for piece in (0, 1):
        from_left[piece] = push(x_block(piece), rows.at[x, c, piece], right)
        from_right[1 - piece] = push(x_block(1 - piece), rows.at[x, c, 1 - piece], left)
    z_slot = slots(4)
    for piece in (0, 1):
        push(x_block(piece), rows.at[4, c, piece], across, z_slot + 2 * c + piece)
    own_sib = [push(x_block(piece), rows.at[x, c, piece], sibling) for piece in (0, 1)]
    own = [pltpu.make_async_copy(x_block(piece), rows.at[x, c, piece], lsem.at[piece]) for piece in (0, 1)]
    for made in own:
        made.start()
    for made in own:
        made.wait()
    for made in own_sib:
        made.wait_recv()

    mine = jnp.where(home, x, 4)
    parts = {}

    def gram_block(i):
        xp = around(x, SHIFTS[i])
        product = lax.dot_general(
            rows[mine].reshape(block, width), rows[xp].reshape(block, width),
            (((1,), (1,)), ((), ())), preferred_element_type=jnp.float32,
        )
        part[i] = (product * (1.0 / n_cols)).astype(jnp.bfloat16).reshape(4, quarter, block)

    def gram_send(i):
        parts[i] = [push(part.at[i, around(y, step)], got.at[i, step - 1], along_y[step - 1]) for step in (1, 2, 3)]

    @pl.when(home)
    def _():
        gram_block(0)

    xl, xr, xo = around(x, 3), around(x, 1), around(x, 2)
    sib = {}
    far = [None, None]
    from_left[0].wait_recv()
    far[0] = push(rows.at[xl, c, 0], rows.at[xl, c, 0], right)
    sib[(3, 0)] = push(rows.at[xl, c, 0], rows.at[xl, c, 0], sibling)
    from_right[1].wait_recv()
    far[1] = push(rows.at[xr, c, 1], rows.at[xr, c, 1], left)
    sib[(1, 1)] = push(rows.at[xr, c, 1], rows.at[xr, c, 1], sibling)
    from_left[1].wait_recv()
    sib[(3, 1)] = push(rows.at[xl, c, 1], rows.at[xl, c, 1], sibling)
    from_right[0].wait_recv()
    sib[(1, 0)] = push(rows.at[xr, c, 0], rows.at[xr, c, 0], sibling)

    @pl.when(jnp.logical_not(home))
    def _():
        for k in range(4):
            pltpu.make_async_remote_copy(
                src_ref=x_block(0), dst_ref=rows.at[4, k // 2, k % 2], send_sem=ssem.at[0],
                recv_sem=rsem.at[z_slot + k], device_id=sibling, device_id_type=MESH,
            ).wait_recv()
        gram_block(0)

    gram_send(0)
    for i in (1, 2):
        for piece in (0, 1):
            sib[(SHIFTS[i], piece)].wait_recv()
        gram_block(i)
        gram_send(i)
    for piece in (0, 1):
        far[piece].wait_recv()
        sib[(2, piece)] = push(rows.at[xo, c, piece], rows.at[xo, c, piece], sibling)
    for piece in (0, 1):
        sib[(2, piece)].wait_recv()
    gram_block(3)
    gram_send(3)

    to_right, to_left, gsib = [], [], []
    zg_slot = slots(8)

    def push_across(i, xs):
        push(gram.at[x, xs, c], gram.at[4, xs, c], across, zg_slot + 2 * i + c)

    for i in range(4):
        for made in parts[i]:
            made.wait_recv()
        xp = around(x, SHIFTS[i])
        total = part[i, y].astype(jnp.float32)
        for step in range(3):
            total += got[i, step].astype(jnp.float32)
        g32[xp] = total
        gram[xp, x, c] = total.astype(jnp.bfloat16)
        to_right.append(push(gram.at[xp, x, c], gram.at[xp, x, c], right))
        to_left.append(push(gram.at[xp, x, c], gram.at[xp, x, c], left))
        gsib.append(push(gram.at[xp, x, c], gram.at[xp, x, c], sibling))
        if i == 0:
            push_across(0, x)

    gfar = []
    for i in range(4):
        for made, xs, onward, keep in ((to_right[i], xl, right, i in (0, 2)), (to_left[i], xr, left, i in (1, 3))):
            made.wait_recv()
            xp = around(xs, SHIFTS[i])
            ref = gram.at[xp, xs, c]
            if keep:
                gfar.append((i, push(ref, ref, onward)))
            if xs is xl and SHIFTS[i] == 1 or xs is xr and SHIFTS[i] == 3:
                push_across(1 if xs is xl else 2, xs)
            gsib.append(push(ref, ref, sibling))
    for i, made in gfar:
        made.wait_recv()
        ref = gram.at[around(xo, SHIFTS[i]), xo, c]
        if SHIFTS[i] == 2:
            push_across(3, xo)
        gsib.append(push(ref, ref, sibling))
    for made in gsib:
        made.wait_recv()

    @pl.when(jnp.logical_not(home))
    def _():
        for k in range(8):
            pltpu.make_async_remote_copy(
                src_ref=gram.at[0, 0, 0], dst_ref=gram.at[4, k // 2, k % 2], send_sem=ssem.at[0],
                recv_sem=rsem.at[zg_slot + k], device_id=sibling, device_id_type=MESH,
            ).wait_recv()

    first = gram[mine].reshape(2 * block, block).T
    for xp in range(4):
        sq[:, :, :, xp * block:(xp + 1) * block] = jnp.dot(
            first, gram[xp].reshape(2 * block, block), preferred_element_type=jnp.float32
        ).astype(jnp.bfloat16).reshape(4, CHUNKS, chunk, block)

    squares = []
    for k in range(CHUNKS):
        squares.append([push(sq.at[around(y, step), k], sgot.at[k, step - 1], along_y[step - 1]) for step in (1, 2, 3)])

    gathers = []

    def mix(k):
        for made in squares[k]:
            made.wait_recv()
        total = sq[y, k].astype(jnp.float32)
        for step in range(3):
            total += sgot[k, step].astype(jnp.float32)
        g = jnp.concatenate([g32[xp, k * chunk:(k + 1) * chunk, :] for xp in range(4)], axis=1)
        mixed[k, y] = (CUBIC * g + QUINTIC * total).astype(jnp.bfloat16)
        gathers.append([push(mixed.at[k, y], mixed.at[k, y], device) for device in along_y])

    y_slot, s_slot = slots(CHUNKS), slots(CHUNKS)
    y_sends, s_sends = [], []

    def multiply(k):
        for made in gathers[k]:
            made.wait_recv()
        lhs = mixed[k].reshape(4 * chunk, 4 * block)
        tile = width // 4
        for t in range(4):
            ypart[k, :, :, :, t * tile:(t + 1) * tile] = jnp.dot(
                lhs, rows[:4, :, :, :, t * tile:(t + 1) * tile].reshape(4 * block, tile), preferred_element_type=jnp.float32
            ).astype(jnp.bfloat16).reshape(2, 2, chunk, tile)
        away = [copy(ypart.at[k, h], yrem.at[0, k], at(z_to=1 - z, c_to=h), y_slot + k) for h in (0, 1)]
        near = copy(ypart.at[k, 1 - c], yrem.at[1, k], sibling, s_slot + k)
        y_sends.append(away)
        s_sends.append(near)

        @pl.when(home)
        def _():
            near.start()

        @pl.when(jnp.logical_not(home))
        def _():
            away[0].start()
            away[1].start()

    for k in range(CHUNKS):
        mix(k)
        if k:
            multiply(k - 1)
    multiply(CHUNKS - 1)

    for k in range(CHUNKS):
        y_sends[k][0].wait_recv()

        @pl.when(jnp.logical_not(home))
        def _():
            s_sends[k].wait_recv()

        for q in range(2):
            near = jnp.where(home, ypart[k, c, q].astype(jnp.float32), yrem[1, k, q].astype(jnp.float32))
            low = q * quarter + k * chunk
            o_ref[low:low + chunk, :] = (
                LINEAR * x_ref[low:low + chunk, :].astype(jnp.float32) + (near + yrem[0, k, q].astype(jnp.float32))
            ).astype(jnp.bfloat16)

    for made in pending:
        made.wait_send()

    @pl.when(home)
    def _():
        for made in s_sends:
            made.wait_send()

    @pl.when(jnp.logical_not(home))
    def _():
        for pair in y_sends:
            for made in pair:
                made.wait_send()


def body(n_cols, iterate):
    height, width = iterate.shape
    half = height // 2
    block = 2 * height
    chunk = half // CHUNKS
    bf16 = jnp.bfloat16
    return pl.pallas_call(
        functools.partial(kernel, n_cols),
        out_shape=jax.ShapeDtypeStruct(iterate.shape, bf16),
        in_specs=[pl.BlockSpec(memory_space=pltpu.VMEM)],
        out_specs=pl.BlockSpec(memory_space=pltpu.VMEM),
        scratch_shapes=[
            pltpu.VMEM((5, 2, 2, half, width), bf16),
            pltpu.VMEM((8, 128), bf16),
            pltpu.VMEM((4, 4, half, block), bf16),
            pltpu.VMEM((4, 3, half, block), bf16),
            pltpu.VMEM((5, 4, 2, half, block), bf16),
            pltpu.VMEM((4, half, block), jnp.float32),
            pltpu.VMEM((4, CHUNKS, chunk, 4 * block), bf16),
            pltpu.VMEM((CHUNKS, 3, chunk, 4 * block), bf16),
            pltpu.VMEM((CHUNKS, 4, chunk, 4 * block), bf16),
            pltpu.VMEM((CHUNKS, 2, 2, chunk, width), bf16),
            pltpu.VMEM((2, CHUNKS, 2, chunk, width), bf16),
            pltpu.SemaphoreType.DMA((128,)),
            pltpu.SemaphoreType.DMA((128,)),
            pltpu.SemaphoreType.DMA((2,)),
        ],
        compiler_params=pltpu.CompilerParams(
            collective_id=0, has_side_effects=True, vmem_limit_bytes=60 * 2**20
        ),
        cost_estimate=pl.CostEstimate(flops=6 * 10**9, bytes_accessed=2 * 10**6, transcendentals=0),
        name="newton_schulz",
    )(iterate)


def solution(mesh):
    spec = P(("expert", "grid"), "layer")

    def run(iterate):
        step = functools.partial(body, iterate.shape[1])
        return jax.shard_map(step, mesh=mesh, in_specs=(spec,), out_specs=spec, check_vma=False)(iterate)

    return run
```

time: 243 us -> 101 us (0.42)
  waiting for transfers between devices: 204 us -> 0 us
  Pallas kernels: 0 us -> 98.8 us
  matrix products: 23.8 us -> 0 us
  between operations: 13.1 us -> 0.01 us
    all_gather x3 -> x0, waiting for transfers between devices: 152 us -> none  [the longest x1 80.6 us: body(): lax.all_gather(iterate, 'grid', axis=0, tiled=True)]
    pallas_call x0 -> x1, Pallas kernels: none -> 98.8 us  [body(): pl.pallas_call(functools.partial(kernel, n_cols), out_shape=jax.ShapeDtyp...]
    reduce_scatter x2 -> x0, waiting for transfers between devices: 51 us -> none  [the longest x1 25.9 us: body(): lax.psum_scatter(partial_value.astype(jnp.bfloat16), 'layer', scatter_dim...]
    dot_general x3 -> x0, matrix products: 23.8 us -> none  [the longest x1 10.2 us: body(): jnp.einsum('ik,jk->ij', iterate, lax.all_gather(iterate, 'grid', axis=0,...]
  transfers between devices with their start and end apart: 5 -> 0, of which waited for: 5 -> 0; matrix products, arithmetic and copies ran while one was open for 0% -> 0% of each run, Pallas kernels for 0% -> 0%
where the time goes in v1:
time: 101 us
  Pallas kernels  98.8 us (98%)
  local copies, waits for them, and re-layouts  2.09 us (2%)
    pallas_call x1, Pallas kernels, body(): pl.pallas_call(functools.partial(kernel, n_cols), out_shape=jax.ShapeDtyp...  98.8 us
    unnamed x1, local copies, waits for them, and re-layouts  2.09 us

profile of v1, /device:TPU:1, one launch (start us, length us, event | category | flops | bytes accessed | tf_op | source)
XLA Modules:
  0.0 100.9 jit_solution(3851728454996186451)
XLA Ops:
  0.0 98.8 %newton_schulz.1 = bf16[192,2048]{1,0:T(8,128)(2,1)} custom-call(bf16[192,2048]{1,0:T(8,128)(2,1)} %x_ref.1), custom_call_target="tpu_custom_call" | custom-call | flops 6000000000 | bytes 2000000 | tf_op jit(solution)/shard_map/newton_schulz/pallas_call | solution.py:285
  98.8 2.1 %copy.3 = bf16[192,2048]{1,0:T(8,128)(2,1)} copy(bf16[192,2048]{1,0:T(8,128)(2,1)} %newton_schulz.1) | data formatting | bytes 1572864

commit v2 on v1

v2 whole, which is shorter than its diff:
```python
import functools

import jax
import jax.numpy as jnp
from jax import lax
from jax.experimental import pallas as pl
from jax.experimental.pallas import tpu as pltpu
from jax.sharding import PartitionSpec as P

MESH = pl.DeviceIdType.MESH

LINEAR = 3.4445
CUBIC = -4.775
QUINTIC = 2.0315

SHIFTS = (0, 1, 3, 2)
CHUNKS = 3
AHEAD = 1
HOLD = 0
PASS_AT = 3


def kernel(
    n_cols, x_ref, o_ref, rows, part, pgot, gram, g32, sq, srel, sacc, sgot, mloc, mixed, ssem, rsem, lsem
):
    half, width = x_ref.shape[0] // 2, x_ref.shape[1]
    quarter = half
    half_q = quarter // 2
    chunk = quarter // CHUNKS
    block = 4 * half
    expert, grid, y = lax.axis_index("expert"), lax.axis_index("grid"), lax.axis_index("layer")
    x, z, c = grid // 4, (grid // 2) % 2, grid % 2
    home = c == z
    visitor = jnp.logical_not(home)

    def at(x_to=None, z_to=None, c_to=None, y_to=None):
        gx = x if x_to is None else x_to
        gz = z if z_to is None else z_to
        gc = c if c_to is None else c_to
        return (expert, gx * 4 + gz * 2 + gc, y if y_to is None else y_to)

    def around(base, step):
        return (base + step) % 4

    up, down, opposite = around(y, 1), around(y, 3), around(y, 2)
    xl, xr, xo = around(x, 3), around(x, 1), around(x, 2)
    right, left = at(x_to=xr), at(x_to=xl)
    sibling = at(c_to=1 - c)
    beyond = at(z_to=1 - z)
    across = at(z_to=1 - z, c_to=z)
    to_up, to_down = at(y_to=up), at(y_to=down)
    taker = y // 2

    barrier = pltpu.get_barrier_semaphore()
    greeted = [right, left, sibling, beyond, at(z_to=1 - z, c_to=1 - c), to_up, to_down]
    greeted += [at(c_to=1 - c, y_to=up), at(c_to=1 - c, y_to=down), at(y_to=opposite), at(x_to=xo)]
    for device in greeted:
        pl.semaphore_signal(barrier, inc=1, device_id=device, device_id_type=MESH)
    pl.semaphore_wait(barrier, len(greeted))

    used = [0, 0]
    pending = []
    guarded = []

    def slots(count=1):
        used[1] += count
        return used[1] - count

    def copy(src, dst, device, slot=None):
        used[0] += 1
        return pltpu.make_async_remote_copy(
            src_ref=src, dst_ref=dst, send_sem=ssem.at[used[0] - 1],
            recv_sem=rsem.at[slots() if slot is None else slot], device_id=device, device_id_type=MESH,
        )

    def push(src, dst, device, slot=None):
        made = copy(src, dst, device, slot)
        made.start()
        pending.append(made)
        return made

    def push_if(condition, copies):
        guarded.append((condition, copies))

        @pl.when(condition)
        def _():
            for made in copies:
                made.start()

    def arrive(ref, slot):
        pltpu.make_async_remote_copy(
            src_ref=ref, dst_ref=ref, send_sem=ssem.at[0], recv_sem=rsem.at[slot],
            device_id=sibling, device_id_type=MESH,
        ).wait_recv()

    def arrive_if(condition, copies):
        @pl.when(condition)
        def _():
            for made in copies:
                made.wait_recv()

    def x_block(core_half):
        return x_ref.at[pl.ds(core_half * half, half), :]

    from_left = [None, None]
    from_right = [None, None]
    for piece in (0, 1):
        from_left[piece] = push(x_block(piece), rows.at[x, c, piece], right)
        from_right[1 - piece] = push(x_block(1 - piece), rows.at[x, c, 1 - piece], left)
    z_slot = slots(4)
    for piece in (0, 1):
        push(x_block(piece), rows.at[4 + x, c, piece], across, z_slot + 2 * c + piece)
    own_sib = [push(x_block(piece), rows.at[x, c, piece], sibling) for piece in (0, 1)]
    own = [pltpu.make_async_copy(x_block(piece), rows.at[x, c, piece], lsem.at[piece]) for piece in (0, 1)]
    for made in own:
        made.start()
    for made in own:
        made.wait()
    for made in own_sib:
        made.wait_recv()

    mine = jnp.where(home, x, 4 + x)

    def gram_block(i):
        xp = around(x, SHIFTS[i])
        product = lax.dot_general(
            rows[mine].reshape(block, width), rows[xp].reshape(block, width),
            (((1,), (1,)), ((), ())), preferred_element_type=jnp.float32,
        )
        part[i] = (product * (1.0 / n_cols)).astype(jnp.bfloat16).reshape(4, quarter, block)

    head, tail = pl.ds(0, half_q), pl.ds(half_q, half_q)
    parts = {}
    for i in range(4):
        parts[i] = [copy(part.at[i, to], pgot.at[i, k], at(y_to=to)) for k, to in enumerate((opposite, up, down))]
        pending.extend(parts[i])

    def gram_send(i):
        for made in parts[i]:
            made.start()

    @pl.when(home)
    def _():
        gram_block(0)
        gram_send(0)

    sib = {}
    far = [None, None]
    from_left[0].wait_recv()
    far[0] = push(rows.at[xl, c, 0], rows.at[xl, c, 0], right)
    sib[(3, 0)] = push(rows.at[xl, c, 0], rows.at[xl, c, 0], sibling)
    from_right[1].wait_recv()
    far[1] = push(rows.at[xr, c, 1], rows.at[xr, c, 1], left)
    sib[(1, 1)] = push(rows.at[xr, c, 1], rows.at[xr, c, 1], sibling)
    from_left[1].wait_recv()
    sib[(3, 1)] = push(rows.at[xl, c, 1], rows.at[xl, c, 1], sibling)
    from_right[0].wait_recv()
    sib[(1, 0)] = push(rows.at[xr, c, 0], rows.at[xr, c, 0], sibling)
    later_z = [push(rows.at[xp, c, piece], rows.at[4 + xp, c, piece], beyond) for xp, piece in ((xl, 0), (xr, 1))]
    to_home = [copy(rows.at[4 + x], rows.at[4 + x], sibling)]

    @pl.when(visitor)
    def _():
        for k in range(4):
            arrive(rows.at[4 + x, k // 2, k % 2], z_slot + k)
        gram_block(0)
        gram_send(0)

    for i in (1, 2):
        for piece in (0, 1):
            sib[(SHIFTS[i], piece)].wait_recv()
        gram_block(i)
        gram_send(i)
    push_if(visitor, to_home)
    for piece in (0, 1):
        far[piece].wait_recv()
        sib[(2, piece)] = push(rows.at[xo, c, piece], rows.at[xo, c, piece], sibling)
    for piece in (0, 1):
        sib[(2, piece)].wait_recv()
    gram_block(3)
    gram_send(3)

    to_right, to_left, gsib, gfar, direct_far = {}, {}, [], [], []
    zg_slot = slots(8)

    def total_block(i):
        for made in parts[i]:
            made.wait_recv()
        xp = around(x, SHIFTS[i])
        total = part[i, y].astype(jnp.float32)
        for k in range(3):
            total += pgot[i, k].astype(jnp.float32)
        g32[xp] = total
        gram[xp, x, c] = total.astype(jnp.bfloat16)
        ref = gram.at[xp, x, c]
        if i == 3:
            direct_far.append(push(ref, ref, at(x_to=xo)))
        to_right[i] = push(ref, ref, right)
        to_left[i] = push(ref, ref, left)
        if i == 0:
            push(ref, gram.at[4, x, c], across, zg_slot + c)
        gsib.append(push(ref, ref, sibling))

    def pass_on(i):
        for made, xs, onward, low, shift in ((to_right[i], xl, right, 0, 1), (to_left[i], xr, left, half_q, 3)):
            made.wait_recv()
            xp = around(xs, SHIFTS[i])
            ref = gram.at[xp, xs, c]
            if i < 3:
                ahead = gram.at[xp, xs, c, pl.ds(low, half_q)]
                gfar.append((i, low, push(ahead, ahead, onward)))
            if SHIFTS[i] == shift:
                push(ref, gram.at[4, xs, c], across, zg_slot + 2 * i + c)
            gsib.append(push(ref, ref, sibling))

    total_block(0)
    total_block(1)
    total_block(2)
    pass_on(0)
    pass_on(1)
    total_block(3)
    pass_on(2)
    for i, low, made in gfar:
        made.wait_recv()
        ref = gram.at[around(xo, SHIFTS[i]), xo, c, pl.ds(low, half_q)]
        gsib.append(push(ref, ref, sibling))
    pass_on(3)
    direct_far[0].wait_recv()
    ref = gram.at[x, xo, c]
    push(ref, gram.at[4, xo, c], across, zg_slot + 6 + c)
    gsib.append(push(ref, ref, sibling))

    sides = ((1, xl, right, 0), (0, xr, left, 1))
    later_x = [copy(rows.at[4 + x, :, p], rows.at[4 + x, :, p], device) for p, _, device, _ in sides]
    later_far = [copy(rows.at[4 + xs, q, p], rows.at[4 + xs, q, p], device) for p, xs, device, q in sides]
    later_home = [copy(rows.at[4 + xs, :, p], rows.at[4 + xs, :, p], sibling) for p, xs, _, _ in sides]
    last_home = [copy(rows.at[4 + xo, q, p], rows.at[4 + xo, q, p], sibling) for p, _, _, q in sides]
    push_if(visitor, later_x)
    last_z = push(rows.at[xo, c, c], rows.at[4 + xo, c, c], beyond)

    for made in gsib:
        made.wait_recv()

    @pl.when(visitor)
    def _():
        for k in range(8):
            arrive(gram.at[0, 0, 0], zg_slot + k)

    first = gram[mine - jnp.where(home, 0, x)].reshape(2 * block, block).T
    for xp in range(4):
        sq[:, :, :, xp * block:(xp + 1) * block] = jnp.dot(
            first, gram[xp].reshape(2 * block, block), preferred_element_type=jnp.float32
        ).astype(jnp.bfloat16).reshape(4, CHUNKS, chunk, block)

    later_sib = []
    for (xp, piece), made in zip(((xl, 0), (xr, 1)), later_z):
        made.wait_recv()
        later_sib.append(push(rows.at[4 + xp, c, piece], rows.at[4 + xp, c, piece], sibling))

    lane = (slice(None), pl.ds(0, 2 * block)), (slice(None), pl.ds(2 * block, 2 * block))
    relay, direct, summed = {}, {}, {}

    def scatter(k):
        relay[k] = [
            push(sq.at[opposite, k, *lane[1]], srel.at[k, 0], to_up),
            push(sq.at[opposite, k, *lane[0]], srel.at[k, 1], to_down),
        ]
        direct[k] = [
            push(sq.at[up, k, *lane[0]], sgot.at[k, 0], to_up),
            push(sq.at[down, k, *lane[1]], sgot.at[k, 1], to_down),
        ]

    def add_on(k):
        summed[k] = []
        for d, (target, device) in enumerate(((up, to_up), (down, to_down))):
            relay[k][d].wait_recv()
            own_part = sq[target, k, :, 2 * block * (1 - d):2 * block * (2 - d)]
            sacc[k, d] = (srel[k, d].astype(jnp.float32) + own_part.astype(jnp.float32)).astype(jnp.bfloat16)
            summed[k].append(push(sacc.at[k, d], sgot.at[k, 2 + d], device))

    near = (slice(None), pl.ds(0, 4 * block))
    other = (slice(None), pl.ds(4 * block, 4 * block))
    takes = c == taker
    takes_down, takes_up, takes_opposite = c == down // 2, c == up // 2, c == opposite // 2
    both = jnp.logical_and
    spread, onward = {}, {}

    def mix(k):
        for made in direct[k] + summed[k]:
            made.wait_recv()
        total = sq[y, k].astype(jnp.float32) + jnp.concatenate(
            [sgot[k, 0].astype(jnp.float32) + sgot[k, 3].astype(jnp.float32),
             sgot[k, 1].astype(jnp.float32) + sgot[k, 2].astype(jnp.float32)], axis=1)
        g = jnp.concatenate([g32[xp, k * chunk:(k + 1) * chunk, :] for xp in range(4)], axis=1)
        value = (CUBIC * g + QUINTIC * total).astype(jnp.bfloat16)
        mloc[k] = value
        src = mloc.at[k]
        spread[k] = dict(
            down_near=copy(src, mixed.at[k, y, *near], at(c_to=taker, y_to=up)),
            up_near=copy(src, mixed.at[k, y, *near], at(c_to=taker, y_to=down)),
            own_near=copy(src, mixed.at[k, y, *near], sibling),
            own_other=copy(src, mixed.at[k, y, *other], at(z_to=1 - z, c_to=taker)),
        )
        push_if(visitor, [spread[k]["own_other"]])
        push_if(home, [spread[k]["down_near"], spread[k]["up_near"]])
        push_if(both(home, jnp.logical_not(takes)), [spread[k]["own_near"]])

        @pl.when(both(home, takes))
        def _():
            mixed[k, y, :, :4 * block] = value

    def spread_other(k):
        arrive_if(takes, [spread[k]["own_other"]])
        ref = mixed.at[k, y, *other]
        onward[k] = dict(down_other=copy(ref, ref, to_up), up_other=copy(ref, ref, to_down))
        push_if(takes, [onward[k]["down_other"], onward[k]["up_other"]])

    def carry(k):
        arrive_if(takes_down, [spread[k]["down_near"]])
        ref = mixed.at[k, down, *near]
        onward[k]["far_near"] = copy(ref, ref, to_up)
        push_if(takes_down, [onward[k]["far_near"]])
        arrive_if(takes_up, [onward[k]["up_other"]])
        ref = mixed.at[k, up, *other]
        onward[k]["far_other"] = copy(ref, ref, to_down)
        push_if(takes_up, [onward[k]["far_other"]])

    def multiply(k):
        arrive_if(takes_down, [onward[k]["down_other"]])
        arrive_if(takes_up, [spread[k]["up_near"]])
        arrive_if(takes_opposite, [onward[k]["far_near"], onward[k]["far_other"]])
        arrive_if(both(takes, visitor), [spread[k]["own_near"]])
        lhs = mixed[k, pl.ds(2 * c, 2)].reshape(2 * chunk, 8 * block)
        tile = width // 4
        for t in range(4):
            cols = slice(t * tile, (t + 1) * tile)
            product = jnp.dot(
                lhs, rows[:, :, :, :, cols].reshape(8 * block, tile), preferred_element_type=jnp.float32
            )
            for q in range(2):
                low = q * quarter + k * chunk
                o_ref[low:low + chunk, cols] = (
                    LINEAR * x_ref[low:low + chunk, cols].astype(jnp.float32) + product[q * chunk:(q + 1) * chunk]
                ).astype(jnp.bfloat16)

    def pass_rows():
        for p in range(2):
            arrive_if(visitor, [later_x[p]])
            push_if(visitor, [later_far[p], later_home[p]])
        last_z.wait_recv()
        later_sib.append(push(rows.at[4 + xo, c, c], rows.at[4 + xo, c, c], sibling))

    def end_rows():
        for p in range(2):
            arrive_if(visitor, [later_far[p]])
            push_if(visitor, [last_home[p]])
        for made in later_sib:
            made.wait_recv()
        arrive_if(home, to_home + later_home + last_home)

    stages = (
        (scatter, 0), (add_on, AHEAD), (mix, AHEAD + 1), (spread_other, AHEAD + 2), (carry, AHEAD + 3),
        (multiply, AHEAD + 4 + HOLD),
    )
    for slot in range(CHUNKS + AHEAD + 4 + HOLD):
        if slot == PASS_AT:
            pass_rows()
        for stage, delay in stages:
            if stage is multiply and slot == delay:
                end_rows()
            if 0 <= slot - delay < CHUNKS:
                stage(slot - delay)

    for made in pending:
        made.wait_send()
    for condition, copies in guarded:

        @pl.when(condition)
        def _():
            for made in copies:
                made.wait_send()


def body(n_cols, iterate):
    height, width = iterate.shape
    half = height // 2
    block = 2 * height
    chunk = half // CHUNKS
    bf16 = jnp.bfloat16
    return pl.pallas_call(
        functools.partial(kernel, n_cols),
        out_shape=jax.ShapeDtypeStruct(iterate.shape, bf16),
        in_specs=[pl.BlockSpec(memory_space=pltpu.VMEM)],
        out_specs=pl.BlockSpec(memory_space=pltpu.VMEM),
        scratch_shapes=[
            pltpu.VMEM((8, 2, 2, half, width), bf16),
            pltpu.VMEM((4, 4, half, block), bf16),
            pltpu.VMEM((4, 3, half, block), bf16),
            pltpu.VMEM((5, 4, 2, half, block), bf16),
            pltpu.VMEM((4, half, block), jnp.float32),
            pltpu.VMEM((4, CHUNKS, chunk, 4 * block), bf16),
            pltpu.VMEM((CHUNKS, 2, chunk, 2 * block), bf16),
            pltpu.VMEM((CHUNKS, 2, chunk, 2 * block), bf16),
            pltpu.VMEM((CHUNKS, 4, chunk, 2 * block), bf16),
            pltpu.VMEM((CHUNKS, chunk, 4 * block), bf16),
            pltpu.VMEM((CHUNKS, 4, chunk, 8 * block), bf16),
            pltpu.SemaphoreType.DMA((256,)),
            pltpu.SemaphoreType.DMA((256,)),
            pltpu.SemaphoreType.DMA((2,)),
        ],
        compiler_params=pltpu.CompilerParams(
            collective_id=0, has_side_effects=True, vmem_limit_bytes=60 * 2**20
        ),
        cost_estimate=pl.CostEstimate(flops=6 * 10**9, bytes_accessed=2 * 10**6, transcendentals=0),
        name="newton_schulz",
    )(iterate)


def solution(mesh):
    spec = P(("expert", "grid"), "layer")

    def run(iterate):
        step = functools.partial(body, iterate.shape[1])
        return jax.shard_map(step, mesh=mesh, in_specs=(spec,), out_specs=spec, check_vma=False)(iterate)

    return run
```

time: 101 us -> 89.5 us (0.89)
  Pallas kernels: 98.8 us -> 87.3 us
    pallas_call x1, Pallas kernels: 98.8 us -> 87.3 us  [body(): pl.pallas_call(functools.partial(kernel, n_cols), out_shape=jax.ShapeDtyp...]
where the time goes in v2:
time: 89.5 us; the launch traced here: 89.4 us
  Pallas kernels  87.3 us (98%)
  local copies, waits for them, and re-layouts  2.09 us (2%)
    pallas_call x1, Pallas kernels, body(): pl.pallas_call(functools.partial(kernel, n_cols), out_shape=jax.ShapeDtyp...  87.3 us
    unnamed x1, local copies, waits for them, and re-layouts  2.09 us

profile of v2, /device:TPU:1, one launch (start us, length us, event | category | flops | bytes accessed | tf_op | source)
XLA Modules:
  0.0 89.4 jit_solution(8728085947492911834)
XLA Ops:
  0.0 87.3 %newton_schulz.1 = bf16[192,2048]{1,0:T(8,128)(2,1)} custom-call(bf16[192,2048]{1,0:T(8,128)(2,1)} %x_ref.1), custom_call_target="tpu_custom_call" | custom-call | flops 6000000000 | bytes 2000000 | tf_op jit(solution)/shard_map/newton_schulz/pallas_call | solution.py:390
  87.3 2.1 %copy.3 = bf16[192,2048]{1,0:T(8,128)(2,1)} copy(bf16[192,2048]{1,0:T(8,128)(2,1)} %newton_schulz.1) | data formatting | bytes 1572864

commit v3 on v2

--- a/solution.py
+++ b/solution.py
@@ -21,7 +21,7 @@
 
 
 def kernel(
-    n_cols, x_ref, o_ref, rows, part, pgot, gram, g32, sq, srel, sacc, sgot, mloc, mixed, ssem, rsem, lsem
+    n_cols, x_ref, o_ref, rows, part, pgot, gram, g32, sq, srel, sacc, sgot, mloc, mixed, result, ssem, rsem, lsem
 ):
     half, width = x_ref.shape[0] // 2, x_ref.shape[1]
     quarter = half
@@ -51,9 +51,17 @@
     to_up, to_down = at(y_to=up), at(y_to=down)
     taker = y // 2
 
+    def x_block(core_half):
+        return x_ref.at[pl.ds(core_half * half, half), :]
+
+    own = [pltpu.make_async_copy(x_block(piece), rows.at[x, c, piece], lsem.at[piece]) for piece in (0, 1)]
+    for made in own:
+        made.start()
+
     barrier = pltpu.get_barrier_semaphore()
     greeted = [right, left, sibling, beyond, at(z_to=1 - z, c_to=1 - c), to_up, to_down]
     greeted += [at(c_to=1 - c, y_to=up), at(c_to=1 - c, y_to=down), at(y_to=opposite), at(x_to=xo)]
+    greeted += [at(z_to=1 - z, c_to=core, y_to=to) for core in (0, 1) for to in (up, down)]
     for device in greeted:
         pl.semaphore_signal(barrier, inc=1, device_id=device, device_id_type=MESH)
     pl.semaphore_wait(barrier, len(greeted))
@@ -98,9 +106,6 @@
         def _():
             for made in copies:
                 made.wait_recv()
-
-    def x_block(core_half):
-        return x_ref.at[pl.ds(core_half * half, half), :]
 
     from_left = [None, None]
     from_right = [None, None]
@@ -111,9 +116,6 @@
     for piece in (0, 1):
         push(x_block(piece), rows.at[4 + x, c, piece], across, z_slot + 2 * c + piece)
     own_sib = [push(x_block(piece), rows.at[x, c, piece], sibling) for piece in (0, 1)]
-    own = [pltpu.make_async_copy(x_block(piece), rows.at[x, c, piece], lsem.at[piece]) for piece in (0, 1)]
-    for made in own:
-        made.start()
     for made in own:
         made.wait()
     for made in own_sib:
@@ -172,14 +174,6 @@
         gram_block(i)
         gram_send(i)
     push_if(visitor, to_home)
-    for piece in (0, 1):
-        far[piece].wait_recv()
-        sib[(2, piece)] = push(rows.at[xo, c, piece], rows.at[xo, c, piece], sibling)
-    for piece in (0, 1):
-        sib[(2, piece)].wait_recv()
-    gram_block(3)
-    gram_send(3)
-
     to_right, to_left, gsib, gfar, direct_far = {}, {}, [], [], []
     zg_slot = slots(8)
 
@@ -193,7 +187,7 @@
         g32[xp] = total
         gram[xp, x, c] = total.astype(jnp.bfloat16)
         ref = gram.at[xp, x, c]
-        if i == 3:
+        if i >= 2:
             direct_far.append(push(ref, ref, at(x_to=xo)))
         to_right[i] = push(ref, ref, right)
         to_left[i] = push(ref, ref, left)
@@ -206,7 +200,7 @@
             made.wait_recv()
             xp = around(xs, SHIFTS[i])
             ref = gram.at[xp, xs, c]
-            if i < 3:
+            if i < 2:
                 ahead = gram.at[xp, xs, c, pl.ds(low, half_q)]
                 gfar.append((i, low, push(ahead, ahead, onward)))
             if SHIFTS[i] == shift:
@@ -215,6 +209,14 @@
 
     total_block(0)
     total_block(1)
+    for piece in (0, 1):
+        far[piece].wait_recv()
+        sib[(2, piece)] = push(rows.at[xo, c, piece], rows.at[xo, c, piece], sibling)
+    for piece in (0, 1):
+        sib[(2, piece)].wait_recv()
+    gram_block(3)
+    gram_send(3)
+
     total_block(2)
     pass_on(0)
     pass_on(1)
@@ -226,6 +228,9 @@
         gsib.append(push(ref, ref, sibling))
     pass_on(3)
     direct_far[0].wait_recv()
+    ref = gram.at[xr, xo, c]
+    gsib.append(push(ref, ref, sibling))
+    direct_far[1].wait_recv()
     ref = gram.at[x, xo, c]
     push(ref, gram.at[4, xo, c], across, zg_slot + 6 + c)
     gsib.append(push(ref, ref, sibling))
@@ -283,7 +288,7 @@
     takes = c == taker
     takes_down, takes_up, takes_opposite = c == down // 2, c == up // 2, c == opposite // 2
     both = jnp.logical_and
-    spread, onward = {}, {}
+    spread, onward, leaving = {}, {}, []
 
     def mix(k):
         for made in direct[k] + summed[k]:
@@ -300,8 +305,10 @@
             up_near=copy(src, mixed.at[k, y, *near], at(c_to=taker, y_to=down)),
             own_near=copy(src, mixed.at[k, y, *near], sibling),
             own_other=copy(src, mixed.at[k, y, *other], at(z_to=1 - z, c_to=taker)),
+            down_other=copy(src, mixed.at[k, y, *other], at(z_to=1 - z, c_to=taker, y_to=up)),
+            up_other=copy(src, mixed.at[k, y, *other], at(z_to=1 - z, c_to=taker, y_to=down)),
         )
-        push_if(visitor, [spread[k]["own_other"]])
+        push_if(visitor, [spread[k][name] for name in ("up_other", "down_other", "own_other")])
         push_if(home, [spread[k]["down_near"], spread[k]["up_near"]])
         push_if(both(home, jnp.logical_not(takes)), [spread[k]["own_near"]])
 
@@ -309,27 +316,23 @@
         def _():
             mixed[k, y, :, :4 * block] = value
 
-    def spread_other(k):
-        arrive_if(takes, [spread[k]["own_other"]])
-        ref = mixed.at[k, y, *other]
-        onward[k] = dict(down_other=copy(ref, ref, to_up), up_other=copy(ref, ref, to_down))
-        push_if(takes, [onward[k]["down_other"], onward[k]["up_other"]])
-
     def carry(k):
         arrive_if(takes_down, [spread[k]["down_near"]])
         ref = mixed.at[k, down, *near]
+        onward[k] = {}
         onward[k]["far_near"] = copy(ref, ref, to_up)
         push_if(takes_down, [onward[k]["far_near"]])
-        arrive_if(takes_up, [onward[k]["up_other"]])
+        arrive_if(takes_up, [spread[k]["up_other"]])
         ref = mixed.at[k, up, *other]
         onward[k]["far_other"] = copy(ref, ref, to_down)
         push_if(takes_up, [onward[k]["far_other"]])
 
     def multiply(k):
-        arrive_if(takes_down, [onward[k]["down_other"]])
+        arrive_if(takes_down, [spread[k]["down_other"]])
         arrive_if(takes_up, [spread[k]["up_near"]])
         arrive_if(takes_opposite, [onward[k]["far_near"], onward[k]["far_other"]])
         arrive_if(both(takes, visitor), [spread[k]["own_near"]])
+        arrive_if(takes, [spread[k]["own_other"]])
         lhs = mixed[k, pl.ds(2 * c, 2)].reshape(2 * chunk, 8 * block)
         tile = width // 4
         for t in range(4):
@@ -339,9 +342,15 @@
             )
             for q in range(2):
                 low = q * quarter + k * chunk
-                o_ref[low:low + chunk, cols] = (
-                    LINEAR * x_ref[low:low + chunk, cols].astype(jnp.float32) + product[q * chunk:(q + 1) * chunk]
+                result[low:low + chunk, cols] = (
+                    LINEAR * rows[x, c, q, k * chunk:(k + 1) * chunk, cols].astype(jnp.float32)
+                    + product[q * chunk:(q + 1) * chunk]
                 ).astype(jnp.bfloat16)
+        for q in range(2):
+            done = pl.ds(q * quarter + k * chunk, chunk)
+            made = pltpu.make_async_copy(result.at[done, :], o_ref.at[done, :], lsem.at[2 + 2 * k + q])
+            made.start()
+            leaving.append(made)
 
     def pass_rows():
         for p in range(2):
@@ -359,10 +368,10 @@
         arrive_if(home, to_home + later_home + last_home)
 
     stages = (
-        (scatter, 0), (add_on, AHEAD), (mix, AHEAD + 1), (spread_other, AHEAD + 2), (carry, AHEAD + 3),
-        (multiply, AHEAD + 4 + HOLD),
+        (scatter, 0), (add_on, AHEAD), (mix, AHEAD + 1), (carry, AHEAD + 2),
+        (multiply, AHEAD + 3 + HOLD),
     )
-    for slot in range(CHUNKS + AHEAD + 4 + HOLD):
+    for slot in range(CHUNKS + AHEAD + 3 + HOLD):
         if slot == PASS_AT:
             pass_rows()
         for stage, delay in stages:
@@ -371,6 +380,8 @@
             if 0 <= slot - delay < CHUNKS:
                 stage(slot - delay)
 
+    for made in leaving:
+        made.wait()
     for made in pending:
         made.wait_send()
     for condition, copies in guarded:
@@ -390,8 +401,8 @@
     return pl.pallas_call(
         functools.partial(kernel, n_cols),
         out_shape=jax.ShapeDtypeStruct(iterate.shape, bf16),
-        in_specs=[pl.BlockSpec(memory_space=pltpu.VMEM)],
-        out_specs=pl.BlockSpec(memory_space=pltpu.VMEM),
+        in_specs=[pl.BlockSpec(memory_space=pl.ANY)],
+        out_specs=pl.BlockSpec(memory_space=pl.ANY),
         scratch_shapes=[
             pltpu.VMEM((8, 2, 2, half, width), bf16),
             pltpu.VMEM((4, 4, half, block), bf16),
@@ -404,9 +415,10 @@
             pltpu.VMEM((CHUNKS, 4, chunk, 2 * block), bf16),
             pltpu.VMEM((CHUNKS, chunk, 4 * block), bf16),
             pltpu.VMEM((CHUNKS, 4, chunk, 8 * block), bf16),
+            pltpu.VMEM(iterate.shape, bf16),
             pltpu.SemaphoreType.DMA((256,)),
             pltpu.SemaphoreType.DMA((256,)),
-            pltpu.SemaphoreType.DMA((2,)),
+            pltpu.SemaphoreType.DMA((2 + 2 * CHUNKS,)),
         ],
         compiler_params=pltpu.CompilerParams(
             collective_id=0, has_side_effects=True, vmem_limit_bytes=60 * 2**20

time: 89.5 us -> 86.7 us (0.969)
  Pallas kernels: 87.3 us -> 84.5 us
    pallas_call x1, Pallas kernels: 87.3 us -> 84.5 us  [body(): pl.pallas_call(functools.partial(kernel, n_cols), out_shape=jax.ShapeDtyp...]
where the time goes in v3:
time: 86.7 us; the launch traced here: 86.6 us
  Pallas kernels  84.5 us (97%)
  local copies, waits for them, and re-layouts  2.09 us (2%)
    pallas_call x1, Pallas kernels, body(): pl.pallas_call(functools.partial(kernel, n_cols), out_shape=jax.ShapeDtyp...  84.5 us
    unnamed x1, local copies, waits for them, and re-layouts  2.09 us

profile of v3, /device:TPU:1, one launch (start us, length us, event | category | flops | bytes accessed | tf_op | source)
XLA Modules:
  0.0 86.6 jit_solution(11718410334883605581)
XLA Ops:
  0.0 84.5 %newton_schulz.1 = bf16[192,2048]{1,0:T(8,128)(2,1)} custom-call(bf16[192,2048]{1,0:T(8,128)(2,1)} %x_ref.1), custom_call_target="tpu_custom_call" | custom-call | flops 6000000000 | bytes 2000000 | tf_op jit(solution)/shard_map/newton_schulz/pallas_call | solution.py:401
  84.5 2.1 %copy.3 = bf16[192,2048]{1,0:T(8,128)(2,1)} copy(bf16[192,2048]{1,0:T(8,128)(2,1)} %newton_schulz.1) | data formatting | bytes 1572864

commit v4 on v3

--- a/solution.py
+++ b/solution.py
@@ -14,7 +14,7 @@
 QUINTIC = 2.0315
 
 SHIFTS = (0, 1, 3, 2)
-CHUNKS = 3
+CHUNKS = 2
 AHEAD = 1
 HOLD = 0
 PASS_AT = 3
@@ -173,7 +173,6 @@
             sib[(SHIFTS[i], piece)].wait_recv()
         gram_block(i)
         gram_send(i)
-    push_if(visitor, to_home)
     to_right, to_left, gsib, gfar, direct_far = {}, {}, [], [], []
     zg_slot = slots(8)
 
@@ -240,7 +239,7 @@
     later_far = [copy(rows.at[4 + xs, q, p], rows.at[4 + xs, q, p], device) for p, xs, device, q in sides]
     later_home = [copy(rows.at[4 + xs, :, p], rows.at[4 + xs, :, p], sibling) for p, xs, _, _ in sides]
     last_home = [copy(rows.at[4 + xo, q, p], rows.at[4 + xo, q, p], sibling) for p, _, _, q in sides]
-    push_if(visitor, later_x)
+    push_if(visitor, later_x + to_home)
     last_z = push(rows.at[xo, c, c], rows.at[4 + xo, c, c], beyond)
 
     for made in gsib:

time: 86.7 us -> 86.9 us (level)
  no operation moved by 1% of the time
where the time goes in v4:
time: 86.9 us; the launch traced here: 86.8 us
  Pallas kernels  84.7 us (97%)
  local copies, waits for them, and re-layouts  2.09 us (2%)
    pallas_call x1, Pallas kernels, body(): pl.pallas_call(functools.partial(kernel, n_cols), out_shape=jax.ShapeDtyp...  84.7 us
    unnamed x1, local copies, waits for them, and re-layouts  2.09 us

profile of v4, /device:TPU:1, one launch (start us, length us, event | category | flops | bytes accessed | tf_op | source)
XLA Modules:
  0.0 86.8 jit_solution(3035296790642828596)
XLA Ops:
  0.0 84.7 %newton_schulz.1 = bf16[192,2048]{1,0:T(8,128)(2,1)} custom-call(bf16[192,2048]{1,0:T(8,128)(2,1)} %x_ref.1), custom_call_target="tpu_custom_call" | custom-call | flops 6000000000 | bytes 2000000 | tf_op jit(solution)/shard_map/newton_schulz/pallas_call | solution.py:400
  84.7 2.1 %copy.3 = bf16[192,2048]{1,0:T(8,128)(2,1)} copy(bf16[192,2048]{1,0:T(8,128)(2,1)} %newton_schulz.1) | data formatting | bytes 1572864
